TPU v7x, 256 devices: a whole 4x4x8 slice. The times are simulated.
256 devices in a mesh: gx: 16 (over z_lo, y), row: 8 (over z_hi, x), ta: 2 (over core).
Axes of the slice: x: 4, y: 4, z: 8 (z_hi: 2, z_lo: 4; z = z_hi * 4 + z_lo), core: 2. Of those that a mesh axis runs over, the one named last changes fastest.
Arguments:
- conserved: float32 [5, 128, 256, 256], P(None, 'gx', 'row', 'ta'), may hold values from -6 to 6
- diffusivity: float32 [5], replicated, may hold values from 0.02 to 0.1
- axial_speed: float32 [5], replicated, may hold values from 0.2 to 0.6
- coupling: float32 [5, 5], replicated, may hold values from -0.6 to 0.6
- pressure_weights: float32 [5], replicated, may hold values from 0.5 to 1.5
- station_cell: int32 [4096], P(('gx', 'row')), may hold values from 0 to 32767, as said below
- owner_row: int32 [4096, 1], P(('gx', 'row')), may hold values from 0 to 7; in each aligned block of 32 rows (0 to 31, 32 to 63, ...) at most 16 rows name the same one
- window_table: int32 [4], replicated, may hold values from 1 to 8
Outputs:
- advanced: float32 [5, 128, 256, 256], P(None, 'gx', 'row', 'ta')
- spectra: float32 [128, 128, 1056], P(('gx', 'row'), 'ta')
Inputs may be any that keep to these rules, and one draw needn't show every extreme that they name: `station_cell`: entries b * 32 to (b + 1) * 32 - 1, with b = g * 8 + j, are distinct cells whose axial index lies in [g * 8, (g + 1) * 8) and radial index in [j * 32, (j + 1) * 32). `owner_row`: in each aligned block of 32 stations, no owner is named more than 16 times.
All inputs are finite; a program needn't handle non-finite values.
Results may differ from a plain program's by a relative error of at most 0.00013.
Values sent between devices are 32-bit elements; how exact they have to be, the bound alone decides.
A program may use at most 64 MiB of HBM per device.

v0:
```python
import functools
import math

import jax
import jax.numpy as jnp
import numpy as np
from jax import lax
from jax.experimental import pallas as pl
from jax.experimental.pallas import tpu as pltpu
from jax.sharding import PartitionSpec as P

NF = 5
CX = 8
CR = 32
LANES = 128
NTH = 256
NM = 33
NFREQ = 16
STEPS = 4
CAP = 16
STN = 32
N_ROW = 8
SLOTS = N_ROW * CAP
COLS = NFREQ * 2 * NM
WIDE = 1152
MESH = pl.DeviceIdType.MESH
F32 = jnp.float32
BF16 = jnp.bfloat16
ORDER = (0, 3, 1, 2)
CHUNKS = 4


def split(value):
    high = value.astype(BF16)
    return high, (value - high.astype(F32)).astype(BF16)


def azimuth_tables():
    theta = np.arange(NTH)
    turns = theta[:, None] * np.arange(NM)[None, :] % NTH
    angle = 2.0 * math.pi / NTH * turns
    table = np.zeros((NTH, LANES), np.float32)
    table[:, :NM] = np.cos(angle) / math.sqrt(NTH)
    table[:, NM : 2 * NM] = np.sin(angle) / math.sqrt(NTH)
    high = table.astype(jnp.bfloat16)
    low = (table - high.astype(np.float32)).astype(jnp.bfloat16)
    high, low = high.reshape(2, LANES, LANES), low.reshape(2, LANES, LANES)
    return np.concatenate([high, high, low], axis=1)


def spread_table():
    spread = np.zeros((LANES, 2, WIDE), np.float32)
    for k in range(NFREQ):
        for part in range(2):
            for m in range(NM):
                column = (k * 2 + part) * NM + m
                spread[m, 0, column] = 1.0
                spread[NM + m, 1, column] = 1.0
    spread = spread.reshape(LANES, 2 * WIDE)
    return np.concatenate([spread, spread], axis=0).astype(jnp.bfloat16)


def phase_rows():
    rows = np.zeros((2 * STEPS, WIDE), np.float32)
    for t in range(STEPS):
        for k in range(NFREQ):
            phase = math.pi * (k + 1) * t / NFREQ
            first = slice((k * 2) * NM, (k * 2 + 1) * NM)
            second = slice((k * 2 + 1) * NM, (k * 2 + 2) * NM)
            rows[t, first] = math.cos(phase)
            rows[STEPS + t, first] = -math.sin(phase)
            rows[t, second] = -math.sin(phase)
            rows[STEPS + t, second] = -math.cos(phase)
    return rows


def kernel(
    n_gx,
    x_ref,
    diffusivity,
    axial_speed,
    coupling,
    weights,
    window,
    cell_ref,
    owner_ref,
    table_hbm,
    spread_hbm,
    phase_ref,
    out_ref,
    spectra_ref,
    s0,
    s1,
    s2,
    s3,
    mirror,
    row_out,
    row_in,
    pressure,
    place,
    table,
    spread,
    z_out,
    z_in,
    acc,
    local_sem,
    gx_send,
    gx_recv,
    ta_send,
    ta_recv,
    row_send,
    row_recv,
    z_send,
    z_recv,
):
    g, j, ta = lax.axis_index("gx"), lax.axis_index("row"), lax.axis_index("ta")
    other = 1 - ta
    state = (s0, s1, s2, s3)
    has = {("gx", 0): g > 0, ("gx", 1): g < n_gx - 1, ("row", 0): j > 0, ("row", 1): j < N_ROW - 1}
    to = {
        ("gx", 0): (g - 1, j, ta),
        ("gx", 1): (g + 1, j, ta),
        ("row", 0): (g, j - 1, ta),
        ("row", 1): (g, j + 1, ta),
    }

    loads = [
        pltpu.make_async_copy(x_ref, s0.at[:, 2 : 2 + CX, 8 : 8 + CR, :], local_sem.at[0]),
        pltpu.make_async_copy(table_hbm.at[ta], table, local_sem.at[1]),
        pltpu.make_async_copy(spread_hbm, spread, local_sem.at[2]),
    ]
    for load in loads:
        load.start()

    barrier = pltpu.get_barrier_semaphore()
    for jj in range(N_ROW):
        for tt in range(2):

            @pl.when(jnp.logical_or(j != jj, ta != tt))
            def _():
                pl.semaphore_signal(barrier, 1, device_id=(g, jj, tt), device_id_type=MESH)

    for side in range(2):

        @pl.when(has["gx", side])
        def _():
            pl.semaphore_signal(barrier, 1, device_id=to["gx", side], device_id_type=MESH)

    for side in range(2):

        @pl.when(jnp.logical_not(has["gx", side]))
        def _():
            for s in state:
                s[:, 10 * side : 10 * side + 2, 8 : 8 + CR, :] = jnp.zeros((NF, 2, CR, LANES), F32)

        @pl.when(jnp.logical_not(has["row", side]))
        def _():
            for t in range(STEPS):
                row_in[t, side] = jnp.zeros((NF, CX, 2, LANES), F32)

    for load in loads:
        load.wait()
    for f in range(NF):
        row_out[0, 0, f] = s0[f, 2 : 2 + CX, 8:10, :]
        row_out[0, 1, f] = s0[f, 2 : 2 + CX, 38:40, :]

    def gx_copy(t, side, c):
        rows = pl.ds(8 + 8 * c, 8)
        return pltpu.make_async_remote_copy(
            src_ref=state[t].at[:, pl.ds(8 * side - 2 * side + 2, 2), rows, :],
            dst_ref=state[t].at[:, pl.ds(10 - 10 * side, 2), rows, :],
            send_sem=gx_send.at[t, side, c],
            recv_sem=gx_recv.at[t, 1 - side, c],
            device_id=to["gx", side],
            device_id_type=MESH,
        )

    def gx_wait(t, side, c):
        rows = pl.ds(8 + 8 * c, 8)
        return pltpu.make_async_remote_copy(
            src_ref=state[t].at[:, pl.ds(2, 2), rows, :],
            dst_ref=state[t].at[:, pl.ds(10 * side, 2), rows, :],
            send_sem=gx_send.at[t, side, c],
            recv_sem=gx_recv.at[t, side, c],
            device_id=to["gx", side],
            device_id_type=MESH,
        )

    def row_copy(t, side):
        return pltpu.make_async_remote_copy(
            src_ref=row_out.at[t, side],
            dst_ref=row_in.at[t, 1 - side],
            send_sem=row_send.at[t, side],
            recv_sem=row_recv.at[t, 1 - side],
            device_id=to["row", side],
            device_id_type=MESH,
        )

    def row_wait(t, side):
        return pltpu.make_async_remote_copy(
            src_ref=row_out.at[t, side],
            dst_ref=row_in.at[t, side],
            send_sem=row_send.at[t, side],
            recv_sem=row_recv.at[t, side],
            device_id=to["row", side],
            device_id_type=MESH,
        )

    def ta_copy(t, c):
        return pltpu.make_async_remote_copy(
            src_ref=state[t].at[:, 2 : 2 + CX, pl.ds(8 + 8 * c, 8), :],
            dst_ref=mirror.at[t, :, :, pl.ds(8 * c, 8), :],
            send_sem=ta_send.at[t, c],
            recv_sem=ta_recv.at[t, c],
            device_id=(g, j, other),
            device_id_type=MESH,
        )

    def send_chunk(t, c):
        for side, edge in ((0, 0), (1, CHUNKS - 1)):
            if c == edge:
                pl.when(has["row", side])(row_copy(t, side).start)
        for side in range(2):
            pl.when(has["gx", side])(gx_copy(t, side, c).start)
        ta_copy(t, c).start()

    peers = 2 * N_ROW - 1 + jnp.where(g > 0, 1, 0) + jnp.where(g < n_gx - 1, 1, 0)
    pl.semaphore_wait(barrier, peers)

    for c in ORDER:
        send_chunk(0, c)

    eye = lax.broadcasted_iota(jnp.int32, (STN, STN), 0) == lax.broadcasted_iota(jnp.int32, (STN, STN), 1)
    before = lax.broadcasted_iota(jnp.int32, (STN, STN), 0) < lax.broadcasted_iota(jnp.int32, (STN, STN), 1)
    owner_across = jnp.broadcast_to(owner_ref[...], (STN, STN)).astype(F32)
    owner_down = jnp.sum(jnp.where(eye, owner_across, 0.0), axis=1, keepdims=True)
    same = jnp.logical_and(before, owner_down == owner_across)
    rank = jnp.sum(jnp.where(same, 1.0, 0.0), axis=0, keepdims=True)
    slot = owner_across[0:1] * float(CAP) + rank
    slots = lax.broadcasted_iota(jnp.int32, (SLOTS, STN), 0).astype(F32)
    slot_onehot = jnp.where(slots == slot, 1.0, 0.0).astype(BF16)
    station = cell_ref[...]
    local_cell = (station // (CR * N_ROW) - g * CX) * CR + (station % (CR * N_ROW) - j * CR)
    cell_across = jnp.broadcast_to(local_cell, (STN, STN)).astype(F32)
    cell_down = jnp.sum(jnp.where(eye, cell_across, 0.0), axis=1, keepdims=True)
    cells = lax.broadcasted_iota(jnp.int32, (STN, CX * CR), 1).astype(F32)
    cell_onehot = jnp.where(cells == cell_down, 1.0, 0.0).astype(BF16)
    place[...] = jnp.dot(slot_onehot, cell_onehot, preferred_element_type=F32).astype(BF16)

    lane = lax.broadcasted_iota(jnp.int32, (8, LANES), 1)
    first1, first2 = lane < 1, lane < 2
    last1, last2 = lane >= LANES - 1, lane >= LANES - 2
    rate = [diffusivity[f] * (1.0 / 12.0) for f in range(NF)]
    velocity = [axial_speed[f] * (1.0 / 12.0) for f in range(NF)]
    mix = [
        [coupling[f, h] + (1.0 - 7.5 * diffusivity[f] if f == h else 0.0) for h in range(NF)]
        for f in range(NF)
    ]
    press = [weights[f] for f in range(NF)]

    def step_chunk(t, c):
        s = state[t]
        r0 = 8 + 8 * c

        def body(x, carry):
            center = [s[f, x + 2, r0 : r0 + 8, :] for f in range(NF)]
            total = None
            for f in range(NF):
                v = center[f]
                o = mirror[t, f, x, 8 * c : 8 * c + 8, :]
                up1, up2 = s[f, x + 3, r0 : r0 + 8, :], s[f, x + 4, r0 : r0 + 8, :]
                dn1, dn2 = s[f, x + 1, r0 : r0 + 8, :], s[f, x, r0 : r0 + 8, :]
                near = (up1 + dn1) + (s[f, x + 2, r0 + 1 : r0 + 9, :] + s[f, x + 2, r0 - 1 : r0 + 7, :])
                far = (up2 + dn2) + (s[f, x + 2, r0 + 2 : r0 + 10, :] + s[f, x + 2, r0 - 2 : r0 + 6, :])
                near = near + (
                    pltpu.roll(jnp.where(first1, o, v), LANES - 1, 1)
                    + pltpu.roll(jnp.where(last1, o, v), 1, 1)
                )
                far = far + (
                    pltpu.roll(jnp.where(first2, o, v), LANES - 2, 1)
                    + pltpu.roll(jnp.where(last2, o, v), 2, 1)
                )
                gradient = 8.0 * (up1 - dn1) - (up2 - dn2)
                new = rate[f] * (16.0 * near - far) - velocity[f] * gradient
                for h in range(NF):
                    new = new + mix[f][h] * center[h]
                if t < STEPS - 1:
                    state[t + 1][f, x + 2, r0 : r0 + 8, :] = new
                    if c == 0:
                        row_out[t + 1, 0, f, x] = new[0:2]
                    if c == CHUNKS - 1:
                        row_out[t + 1, 1, f, x] = new[6:8]
                else:
                    out_ref[f, x, 8 * c : 8 * c + 8, :] = new
                part = press[f] * new
                total = part if total is None else total + part
            pressure[pl.ds(x * CR + 8 * c, 8), :] = total
            return carry

        lax.fori_loop(0, CX, body, 0)

    def coefficients(t):
        high, low = split(pressure[...])
        both = jnp.dot(place[...], jnp.concatenate([high, low], axis=1), preferred_element_type=F32)
        high, low = split(both[:, :LANES] + both[:, LANES:])
        z_out[t] = jnp.dot(
            jnp.concatenate([high, low, high], axis=1), table[...], preferred_element_type=F32
        ).reshape(N_ROW, CAP, LANES)

    half = j // (N_ROW // 2)
    source = (j % (N_ROW // 2)) * 2 + ta
    groups = ((0, STEPS - 1), (STEPS - 1, 1))

    def z_copy(group, owner):
        first, count = groups[group]
        return pltpu.make_async_remote_copy(
            src_ref=z_out.at[pl.ds(first, count), owner],
            dst_ref=z_in.at[source, pl.ds(first, count)],
            send_sem=z_send.at[group, owner],
            recv_sem=z_recv.at[group, source],
            device_id=(g, owner, half),
            device_id_type=MESH,
        )

    def away(owner):
        return jnp.logical_or(owner != j, half != ta)

    def z_start(group):
        for owner in range(N_ROW):
            pl.when(away(owner))(z_copy(group, owner).start)

        @pl.when(half == ta)
        def _():
            first, count = groups[group]
            for t in range(first, first + count):
                z_in[source, t] = z_out[t, j]

    def z_wait(group):
        first, count = groups[group]
        for src in range(N_ROW):
            copy = pltpu.make_async_remote_copy(
                src_ref=z_out.at[pl.ds(first, count), 0],
                dst_ref=z_in.at[src, pl.ds(first, count)],
                send_sem=z_send.at[group, 0],
                recv_sem=z_recv.at[group, src],
                device_id=(g, j, other),
                device_id_type=MESH,
            )
            mine = jnp.logical_and(half == ta, source == src)
            pl.when(jnp.logical_not(mine))(copy.wait_recv)

    def accumulate(t, start):
        w = window[t].astype(F32) * 0.125
        z = jnp.concatenate([z_in[2 * i, t] + z_in[2 * i + 1, t] for i in range(N_ROW // 2)], axis=0)
        high, low = split(z * w)
        wide = jnp.dot(jnp.concatenate([high, low], axis=1), spread[...], preferred_element_type=F32)
        new = phase_ref[t : t + 1, :] * wide[:, :WIDE] + phase_ref[STEPS + t : STEPS + t + 1, :] * wide[:, WIDE:]
        return new if start is None else start + new

    for t in range(STEPS):
        for c in ORDER:
            for side, edge in ((0, 0), (1, CHUNKS - 1)):
                if c == edge:
                    pl.when(has["row", side])(row_wait(t, side).wait_recv)
                    at = 6 if side == 0 else 8 + CR
                    for f in range(NF):
                        state[t][f, 2 : 2 + CX, at : at + 2, :] = row_in[t, side, f]
            for side in range(2):
                pl.when(has["gx", side])(gx_wait(t, side, c).wait_recv)
            ta_copy(t, c).wait_recv()
            step_chunk(t, c)
            if t < STEPS - 1:
                send_chunk(t + 1, c)
        coefficients(t)
        if t == STEPS - 2:
            z_start(0)
    z_start(1)
    z_wait(0)
    total = None
    for t in range(STEPS - 1):
        total = accumulate(t, total)
    acc[...] = total
    for t in range(STEPS):
        for c in range(CHUNKS):
            for side in range(2):
                pl.when(has["gx", side])(gx_copy(t, side, c).wait_send)
            ta_copy(t, c).wait_send()
        for side in range(2):
            pl.when(has["row", side])(row_copy(t, side).wait_send)
    for group in range(2):
        for owner in range(N_ROW):
            pl.when(away(owner))(z_copy(group, owner).wait_send)
    z_wait(1)
    spectra_ref[...] = accumulate(STEPS - 1, acc[...])[:, :COLS]


def local(n_gx, conserved, diffusivity, axial_speed, coupling, weights, station_cell, owner_row, window):
    smem = pl.BlockSpec(memory_space=pltpu.SMEM)
    vmem = pl.BlockSpec(memory_space=pltpu.VMEM)
    anywhere = pl.BlockSpec(memory_space=pl.ANY)
    big = pltpu.VMEM((NF, CX + 4, CR + 16, LANES), F32)
    dma = pltpu.SemaphoreType.DMA
    advanced, spectra = pl.pallas_call(
        functools.partial(kernel, n_gx),
        out_shape=(
            jax.ShapeDtypeStruct((NF, CX, CR, LANES), F32),
            jax.ShapeDtypeStruct((SLOTS // 2, COLS), F32),
        ),
        in_specs=[anywhere] + [smem] * 5 + [vmem] * 2 + [anywhere] * 2 + [vmem],
        out_specs=(vmem, vmem),
        scratch_shapes=[
            big,
            big,
            big,
            big,
            pltpu.VMEM((STEPS, NF, CX, CR, LANES), F32),
            pltpu.VMEM((STEPS, 2, NF, CX, 2, LANES), F32),
            pltpu.VMEM((STEPS, 2, NF, CX, 2, LANES), F32),
            pltpu.VMEM((CX * CR, LANES), F32),
            pltpu.VMEM((SLOTS, CX * CR), BF16),
            pltpu.VMEM((3 * LANES, LANES), BF16),
            pltpu.VMEM((2 * LANES, 2 * WIDE), BF16),
            pltpu.VMEM((STEPS, N_ROW, CAP, LANES), F32),
            pltpu.VMEM((N_ROW, STEPS, CAP, LANES), F32),
            pltpu.VMEM((SLOTS // 2, WIDE), F32),
            dma((3,)),
            dma((STEPS, 2, CHUNKS)),
            dma((STEPS, 2, CHUNKS)),
            dma((STEPS, CHUNKS)),
            dma((STEPS, CHUNKS)),
            dma((STEPS, 2)),
            dma((STEPS, 2)),
            dma((2, N_ROW)),
            dma((2, N_ROW)),
        ],
        compiler_params=pltpu.CompilerParams(
            collective_id=0, has_side_effects=True, vmem_limit_bytes=40 * 1024 * 1024
        ),
    )(
        conserved,
        diffusivity,
        axial_speed,
        coupling,
        weights,
        window,
        station_cell.reshape(1, STN),
        owner_row.reshape(1, STN),
        jnp.asarray(azimuth_tables()),
        jnp.asarray(spread_table()),
        jnp.asarray(phase_rows()),
    )
    return advanced, spectra[None]


def solution(mesh):
    in_specs = (
        P(None, "gx", "row", "ta"),
        P(),
        P(),
        P(),
        P(),
        P(("gx", "row")),
        P(("gx", "row"), None),
        P(),
    )
    out_specs = (P(None, "gx", "row", "ta"), P(("gx", "row"), "ta", None))
    return jax.shard_map(
        functools.partial(local, mesh.shape["gx"]),
        mesh=mesh,
        in_specs=in_specs,
        out_specs=out_specs,
        check_vma=False,
    )
```

profile of v0, /device:TPU:39, one launch (start us, length us, event | category | flops | bytes accessed | tf_op | source)
XLA Modules:
  0.0 60.1 jit_solution(12616153858718417784)
XLA Ops:
  0.6 0.0 copy-start
  0.6 1.3 %copy-done = bf16[256,2304]{1,0:T(8,128)(2,1)S(1)} copy-done((bf16[256,2304]{1,0:T(8,128)(2,1)S(1)}, bf16[256,2304]{1,0:T(8,128)(2,1)}, u32[]{:S(2)}) %copy-start) | copy-done | bytes 1179672
  1.9 0.0 copy-start.1
  1.9 1.1 %copy-done.1 = f32[5,8,32,128]{3,2,1,0:T(8,128)S(1)} copy-done((f32[5,8,32,128]{3,2,1,0:T(8,128)S(1)}, f32[5,8,32,128]{3,2,1,0:T(8,128)}, u32[]{:S(2)}) %copy-start.1) | copy-done | bytes 655384
  3.0 0.0 copy-start.2
  3.0 0.9 %copy-done.2 = bf16[2,384,128]{2,1,0:T(8,128)(2,1)S(1)} copy-done((bf16[2,384,128]{2,1,0:T(8,128)(2,1)S(1)}, bf16[2,384,128]{2,1,0:T(8,128)(2,1)}, u32[]{:S(2)}) %copy-start.2) | copy-done | bytes 196632
  3.9 0.0 copy-start.3
  3.9 0.8 %copy-done.3 = f32[8,1152]{1,0:T(8,128)S(1)} copy-done((f32[8,1152]{1,0:T(8,128)S(1)}, f32[8,1152]{1,0:T(8,128)}, u32[]{:S(2)}) %copy-start.3) | copy-done | bytes 36888
  4.7 0.0 copy-start.4
  4.7 0.7 %copy-done.4 = f32[5,5]{1,0:T(8,128)S(1)} copy-done((f32[5,5]{1,0:T(8,128)S(1)}, f32[5,5]{1,0:T(8,128)}, u32[]{:S(2)}) %copy-start.4) | copy-done | bytes 124
  5.4 0.0 copy-start.5
  5.4 0.7 %copy-done.5 = f32[5]{0:T(128)S(1)} copy-done((f32[5]{0:T(128)S(1)}, f32[5]{0:T(128)}, u32[]{:S(2)}) %copy-start.5) | copy-done | bytes 44
  6.0 0.0 copy-start.6
  6.0 0.7 %copy-done.6 = f32[5]{0:T(128)S(1)} copy-done((f32[5]{0:T(128)S(1)}, f32[5]{0:T(128)}, u32[]{:S(2)}) %copy-start.6) | copy-done | bytes 44
  6.7 0.0 copy-start.7
  6.7 0.7 %copy-done.7 = f32[5]{0:T(128)S(1)} copy-done((f32[5]{0:T(128)S(1)}, f32[5]{0:T(128)}, u32[]{:S(2)}) %copy-start.7) | copy-done | bytes 44
  7.3 0.0 copy-start.8
  7.3 0.7 %copy-done.8 = s32[4]{0:T(128)S(1)} copy-done((s32[4]{0:T(128)S(1)}, s32[4]{0:T(128)}, u32[]{:S(2)}) %copy-start.8) | copy-done | bytes 40
  8.0 0.0 copy-start.9
  8.0 0.7 %copy-done.9 = s32[32]{0:T(128)S(1)} copy-done((s32[32]{0:T(128)S(1)}, s32[32]{0:T(128)}, u32[]{:S(2)}) %copy-start.9) | copy-done | bytes 152
  8.7 0.7 %copy-done.10 = s32[32,1]{0,1:T(1,128)S(1)} copy-done((s32[32,1]{0,1:T(1,128)S(1)}, s32[32,1]{0,1:T(1,128)}, u32[]{:S(2)}) %copy-start.10) | copy-done | bytes 152
  9.3 49.2 %shard_map.122 = (f32[5,8,32,128]{3,2,1,0:T(8,128)S(1)}, f32[64,1056]{1,0:T(8,128)S(1)}) custom-call(f32[5,8,32,128]{3,2,1,0:T(8,128)S(1)} %copy-done.1, f32[5]{0:T(128)S(1)} %copy-done.5, f32[5]{0:T(128)S(1)} %copy-done.6, f32[5,5]{1,0:T(8,128)S(1)} %copy-done.4, f32[5]{0:T(128)S(1)} %copy-done.7, s32[4]{0:T(128)S(1)} %copy-done.8, s32[1,32]{1,0:T(1,128)S(1)} %bitcast.4, ...), custom_call_target="tpu_custom_call" | custom-call | tf_op jit(solution)/shard_map/pallas_call | solution.py:403
  58.5 0.8 %copy.15 = f32[5,8,32,128]{3,2,1,0:T(8,128)} copy(f32[5,8,32,128]{3,2,1,0:T(8,128)S(1)} %get-tuple-element.8) | data formatting | bytes 1310720
  59.3 0.7 %copy.16 = f32[1,64,1056]{2,1,0:T(8,128)} copy(f32[1,64,1056]{2,1,0:T(8,128)S(1)} %bitcast.3) | data formatting | bytes 540672
  (1 shorter events, 0.0 us)
Async XLA Ops:
  0.6 1.3 %copy-start = (bf16[256,2304]{1,0:T(8,128)(2,1)S(1)}, bf16[256,2304]{1,0:T(8,128)(2,1)}, u32[]{:S(2)}) copy-start(bf16[256,2304]{1,0:T(8,128)(2,1)} %constant.7.clone.spread_hbm) | copy-start | bytes 3538948
  1.9 1.1 %copy-start.1 = (f32[5,8,32,128]{3,2,1,0:T(8,128)S(1)}, f32[5,8,32,128]{3,2,1,0:T(8,128)}, u32[]{:S(2)}) copy-start(f32[5,8,32,128]{3,2,1,0:T(8,128)} %x_ref.1) | copy-start | bytes 1966084
  3.0 0.9 %copy-start.2 = (bf16[2,384,128]{2,1,0:T(8,128)(2,1)S(1)}, bf16[2,384,128]{2,1,0:T(8,128)(2,1)}, u32[]{:S(2)}) copy-start(bf16[2,384,128]{2,1,0:T(8,128)(2,1)} %constant.6.clone.table_hbm) | copy-start | bytes 589828
  3.9 0.8 %copy-start.3 = (f32[8,1152]{1,0:T(8,128)S(1)}, f32[8,1152]{1,0:T(8,128)}, u32[]{:S(2)}) copy-start(f32[8,1152]{1,0:T(8,128)} %constant.8.clone.phase_ref) | copy-start | bytes 110596
  4.7 0.7 %copy-start.4 = (f32[5,5]{1,0:T(8,128)S(1)}, f32[5,5]{1,0:T(8,128)}, u32[]{:S(2)}) copy-start(f32[5,5]{1,0:T(8,128)} %coupling.1) | copy-start | bytes 304
  5.4 0.7 %copy-start.5 = (f32[5]{0:T(128)S(1)}, f32[5]{0:T(128)}, u32[]{:S(2)}) copy-start(f32[5]{0:T(128)} %diffusivity.1) | copy-start | bytes 64
  6.0 0.7 %copy-start.6 = (f32[5]{0:T(128)S(1)}, f32[5]{0:T(128)}, u32[]{:S(2)}) copy-start(f32[5]{0:T(128)} %axial_speed.1) | copy-start | bytes 64
  6.7 0.7 %copy-start.7 = (f32[5]{0:T(128)S(1)}, f32[5]{0:T(128)}, u32[]{:S(2)}) copy-start(f32[5]{0:T(128)} %weights.1) | copy-start | bytes 64
  7.3 0.7 %copy-start.8 = (s32[4]{0:T(128)S(1)}, s32[4]{0:T(128)}, u32[]{:S(2)}) copy-start(s32[4]{0:T(128)} %window.1) | copy-start | bytes 52
  8.0 0.7 %copy-start.9 = (s32[32]{0:T(128)S(1)}, s32[32]{0:T(128)}, u32[]{:S(2)}) copy-start(s32[32]{0:T(128)} %param.16) | copy-start | bytes 388
  8.7 0.7 %copy-start.10 = (s32[32,1]{0,1:T(1,128)S(1)}, s32[32,1]{0,1:T(1,128)}, u32[]{:S(2)}) copy-start(s32[32,1]{0,1:T(1,128)} %param.17) | copy-start | bytes 388
where the time goes:
time: 60.4 us; the launch traced here: 60.1 us
  Pallas kernels  49.2 us (81%)
  local copies, waits for them, and re-layouts  10.2 us (17%)
  between operations  0.66 us (1%)
    pallas_call x1, Pallas kernels, local(): pl.pallas_call(functools.partial(kernel, n_gx), out_shape=(jax.ShapeDtype...  49.2 us
    unnamed x24, local copies, waits for them, and re-layouts  10.2 us

commit v1 on v0

--- a/solution.py
+++ b/solution.py
@@ -77,16 +77,16 @@
 def kernel(
     n_gx,
     x_ref,
-    diffusivity,
-    axial_speed,
-    coupling,
-    weights,
-    window,
-    cell_ref,
-    owner_ref,
+    diffusivity_hbm,
+    axial_speed_hbm,
+    coupling_hbm,
+    weights_hbm,
+    window_hbm,
+    cell_hbm,
+    owner_hbm,
     table_hbm,
     spread_hbm,
-    phase_ref,
+    phase_hbm,
     out_ref,
     spectra_ref,
     s0,
@@ -100,6 +100,14 @@
     place,
     table,
     spread,
+    phase_ref,
+    cell_ref,
+    owner_ref,
+    diffusivity,
+    axial_speed,
+    coupling,
+    weights,
+    window,
     z_out,
     z_in,
     acc,
@@ -128,6 +136,14 @@
         pltpu.make_async_copy(x_ref, s0.at[:, 2 : 2 + CX, 8 : 8 + CR, :], local_sem.at[0]),
         pltpu.make_async_copy(table_hbm.at[ta], table, local_sem.at[1]),
         pltpu.make_async_copy(spread_hbm, spread, local_sem.at[2]),
+        pltpu.make_async_copy(phase_hbm, phase_ref, local_sem.at[3]),
+        pltpu.make_async_copy(cell_hbm, cell_ref, local_sem.at[4]),
+        pltpu.make_async_copy(owner_hbm, owner_ref, local_sem.at[5]),
+        pltpu.make_async_copy(diffusivity_hbm, diffusivity, local_sem.at[6]),
+        pltpu.make_async_copy(axial_speed_hbm, axial_speed, local_sem.at[7]),
+        pltpu.make_async_copy(coupling_hbm, coupling, local_sem.at[8]),
+        pltpu.make_async_copy(weights_hbm, weights, local_sem.at[9]),
+        pltpu.make_async_copy(window_hbm, window, local_sem.at[10]),
     ]
     for load in loads:
         load.start()
@@ -158,8 +174,7 @@
             for t in range(STEPS):
                 row_in[t, side] = jnp.zeros((NF, CX, 2, LANES), F32)
 
-    for load in loads:
-        load.wait()
+    loads[0].wait()
     for f in range(NF):
         row_out[0, 0, f] = s0[f, 2 : 2 + CX, 8:10, :]
         row_out[0, 1, f] = s0[f, 2 : 2 + CX, 38:40, :]
@@ -229,6 +244,9 @@
 
     for c in ORDER:
         send_chunk(0, c)
+
+    for load in loads[1:]:
+        load.wait()
 
     eye = lax.broadcasted_iota(jnp.int32, (STN, STN), 0) == lax.broadcasted_iota(jnp.int32, (STN, STN), 1)
     before = lax.broadcasted_iota(jnp.int32, (STN, STN), 0) < lax.broadcasted_iota(jnp.int32, (STN, STN), 1)
@@ -297,7 +315,7 @@
             pressure[pl.ds(x * CR + 8 * c, 8), :] = total
             return carry
 
-        lax.fori_loop(0, CX, body, 0)
+        lax.fori_loop(0, CX, body, 0, unroll=True)
 
     def coefficients(t):
         high, low = split(pressure[...])
@@ -395,9 +413,8 @@
 
 
 def local(n_gx, conserved, diffusivity, axial_speed, coupling, weights, station_cell, owner_row, window):
-    smem = pl.BlockSpec(memory_space=pltpu.SMEM)
     vmem = pl.BlockSpec(memory_space=pltpu.VMEM)
-    anywhere = pl.BlockSpec(memory_space=pl.ANY)
+    hbm = pl.BlockSpec(memory_space=pltpu.HBM)
     big = pltpu.VMEM((NF, CX + 4, CR + 16, LANES), F32)
     dma = pltpu.SemaphoreType.DMA
     advanced, spectra = pl.pallas_call(
@@ -406,7 +423,7 @@
             jax.ShapeDtypeStruct((NF, CX, CR, LANES), F32),
             jax.ShapeDtypeStruct((SLOTS // 2, COLS), F32),
         ),
-        in_specs=[anywhere] + [smem] * 5 + [vmem] * 2 + [anywhere] * 2 + [vmem],
+        in_specs=[hbm] * 11,
         out_specs=(vmem, vmem),
         scratch_shapes=[
             big,
@@ -420,10 +437,18 @@
             pltpu.VMEM((SLOTS, CX * CR), BF16),
             pltpu.VMEM((3 * LANES, LANES), BF16),
             pltpu.VMEM((2 * LANES, 2 * WIDE), BF16),
+            pltpu.VMEM((2 * STEPS, WIDE), F32),
+            pltpu.VMEM((1, STN), jnp.int32),
+            pltpu.VMEM((1, STN), jnp.int32),
+            pltpu.SMEM((NF,), F32),
+            pltpu.SMEM((NF,), F32),
+            pltpu.SMEM((NF, NF), F32),
+            pltpu.SMEM((NF,), F32),
+            pltpu.SMEM((STEPS,), jnp.int32),
             pltpu.VMEM((STEPS, N_ROW, CAP, LANES), F32),
             pltpu.VMEM((N_ROW, STEPS, CAP, LANES), F32),
             pltpu.VMEM((SLOTS // 2, WIDE), F32),
-            dma((3,)),
+            dma((11,)),
             dma((STEPS, 2, CHUNKS)),
             dma((STEPS, 2, CHUNKS)),
             dma((STEPS, CHUNKS)),
@@ -437,17 +462,22 @@
             collective_id=0, has_side_effects=True, vmem_limit_bytes=40 * 1024 * 1024
         ),
     )(
-        conserved,
-        diffusivity,
-        axial_speed,
-        coupling,
-        weights,
-        window,
-        station_cell.reshape(1, STN),
-        owner_row.reshape(1, STN),
-        jnp.asarray(azimuth_tables()),
-        jnp.asarray(spread_table()),
-        jnp.asarray(phase_rows()),
+        *(
+            pltpu.with_memory_space_constraint(operand, pltpu.HBM)
+            for operand in (
+                conserved,
+                diffusivity,
+                axial_speed,
+                coupling,
+                weights,
+                window,
+                station_cell.reshape(1, STN),
+                owner_row.reshape(1, STN),
+                jnp.asarray(azimuth_tables()),
+                jnp.asarray(spread_table()),
+                jnp.asarray(phase_rows()),
+            )
+        )
     )
     return advanced, spectra[None]
 

time: 60.4 us -> 48.3 us (0.80)
  local copies, waits for them, and re-layouts: 10.2 us -> 1.55 us
  Pallas kernels: 49.2 us -> 46 us
    unnamed x24 -> x2, local copies, waits for them, and re-layouts: 10.2 us -> 1.55 us
    pallas_call x1, Pallas kernels: 49.2 us -> 46 us  [local(): pl.pallas_call(functools.partial(kernel, n_gx), out_shape=(jax.ShapeDtype...]
where the time goes in v1:
time: 48.3 us; the launch traced here: 48.2 us
  Pallas kernels  46 us (95%)
  local copies, waits for them, and re-layouts  1.55 us (3%)
  between operations  0.64 us (1%)
    pallas_call x1, Pallas kernels, local(): pl.pallas_call(functools.partial(kernel, n_gx), out_shape=(jax.ShapeDtype...  46 us
    unnamed x2, local copies, waits for them, and re-layouts  1.55 us

profile of v1, /device:TPU:39, one launch (start us, length us, event | category | flops | bytes accessed | tf_op | source)
XLA Modules:
  0.0 48.2 jit_solution(15364786950450539075)
XLA Ops:
  0.6 46.0 %shard_map.122 = (f32[5,8,32,128]{3,2,1,0:T(8,128)S(1)}, f32[64,1056]{1,0:T(8,128)S(1)}) custom-call(f32[5,8,32,128]{3,2,1,0:T(8,128)} %x_ref.1, f32[5]{0:T(128)} %diffusivity_hbm.1, f32[5]{0:T(128)} %axial_speed_hbm.1, f32[5,5]{1,0:T(8,128)} %coupling_hbm.1, f32[5]{0:T(128)} %weights_hbm.1, s32[4]{0:T(128)} %window_hbm.1, s32[1,32]{1,0:T(1,128)} %bitcast.4, ...), custom_call_target="tpu_custom_call" | custom-call | tf_op jit(solution)/shard_map/pallas_call | solution.py:420
  46.7 0.8 %copy.15 = f32[5,8,32,128]{3,2,1,0:T(8,128)} copy(f32[5,8,32,128]{3,2,1,0:T(8,128)S(1)} %get-tuple-element.8) | data formatting | bytes 1310720
  47.5 0.7 %copy.16 = f32[1,64,1056]{2,1,0:T(8,128)} copy(f32[1,64,1056]{2,1,0:T(8,128)S(1)} %bitcast.3) | data formatting | bytes 540672

commit v2 on v1

--- a/solution.py
+++ b/solution.py
@@ -21,6 +21,7 @@
 STN = 32
 N_ROW = 8
 SLOTS = N_ROW * CAP
+HALF = SLOTS // 2
 COLS = NFREQ * 2 * NM
 WIDE = 1152
 MESH = pl.DeviceIdType.MESH
@@ -35,43 +36,42 @@
     return high, (value - high.astype(F32)).astype(BF16)
 
 
+def in_pieces(table, axis):
+    high = table.astype(jnp.bfloat16)
+    low = (table - high.astype(np.float32)).astype(jnp.bfloat16)
+    return np.concatenate([high, high, low], axis=axis)
+
+
+def lane_of(t, part, m):
+    return (0 if t == STEPS - 1 else 2 * NM * t) + NM * part + m
+
+
 def azimuth_tables():
     theta = np.arange(NTH)
     turns = theta[:, None] * np.arange(NM)[None, :] % NTH
     angle = 2.0 * math.pi / NTH * turns
-    table = np.zeros((NTH, LANES), np.float32)
-    table[:, :NM] = np.cos(angle) / math.sqrt(NTH)
-    table[:, NM : 2 * NM] = np.sin(angle) / math.sqrt(NTH)
-    high = table.astype(jnp.bfloat16)
-    low = (table - high.astype(np.float32)).astype(jnp.bfloat16)
-    high, low = high.reshape(2, LANES, LANES), low.reshape(2, LANES, LANES)
-    return np.concatenate([high, high, low], axis=1)
-
-
-def spread_table():
-    spread = np.zeros((LANES, 2, WIDE), np.float32)
-    for k in range(NFREQ):
-        for part in range(2):
-            for m in range(NM):
-                column = (k * 2 + part) * NM + m
-                spread[m, 0, column] = 1.0
-                spread[NM + m, 1, column] = 1.0
-    spread = spread.reshape(LANES, 2 * WIDE)
-    return np.concatenate([spread, spread], axis=0).astype(jnp.bfloat16)
-
-
-def phase_rows():
-    rows = np.zeros((2 * STEPS, WIDE), np.float32)
+    table = np.zeros((STEPS, NTH, 2 * LANES), np.float32)
     for t in range(STEPS):
+        table[t, :, lane_of(t, 0, 0) : lane_of(t, 0, NM)] = np.cos(angle) / math.sqrt(NTH)
+        table[t, :, lane_of(t, 1, 0) : lane_of(t, 1, NM)] = np.sin(angle) / math.sqrt(NTH)
+    table = table.reshape(STEPS, 2, LANES, 2 * LANES).swapaxes(0, 1)
+    return in_pieces(table, 2)
+
+
+def phase_tables():
+    early = np.zeros((2 * LANES, WIDE), np.float32)
+    late = np.zeros((LANES, WIDE), np.float32)
+    for t in range(STEPS):
+        rows = late if t == STEPS - 1 else early
         for k in range(NFREQ):
             phase = math.pi * (k + 1) * t / NFREQ
-            first = slice((k * 2) * NM, (k * 2 + 1) * NM)
-            second = slice((k * 2 + 1) * NM, (k * 2 + 2) * NM)
-            rows[t, first] = math.cos(phase)
-            rows[STEPS + t, first] = -math.sin(phase)
-            rows[t, second] = -math.sin(phase)
-            rows[STEPS + t, second] = -math.cos(phase)
-    return rows
+            for m in range(NM):
+                first, second = (k * 2) * NM + m, (k * 2 + 1) * NM + m
+                rows[lane_of(t, 0, m), first] = math.cos(phase)
+                rows[lane_of(t, 1, m), first] = -math.sin(phase)
+                rows[lane_of(t, 0, m), second] = -math.sin(phase)
+                rows[lane_of(t, 1, m), second] = -math.cos(phase)
+    return in_pieces(early, 0), in_pieces(late, 0)
 
 
 def kernel(
@@ -85,8 +85,8 @@
     cell_hbm,
     owner_hbm,
     table_hbm,
-    spread_hbm,
-    phase_hbm,
+    early_hbm,
+    late_hbm,
     out_ref,
     spectra_ref,
     s0,
@@ -99,8 +99,8 @@
     pressure,
     place,
     table,
-    spread,
-    phase_ref,
+    early,
+    late,
     cell_ref,
     owner_ref,
     diffusivity,
@@ -108,9 +108,16 @@
     coupling,
     weights,
     window,
-    z_out,
-    z_in,
+    z_early,
+    z_late,
+    half_early,
+    half_late,
+    sum_early,
+    sum_late,
+    in_early,
+    in_late,
     acc,
+    ready,
     local_sem,
     gx_send,
     gx_recv,
@@ -118,6 +125,8 @@
     ta_recv,
     row_send,
     row_recv,
+    half_send,
+    half_recv,
     z_send,
     z_recv,
 ):
@@ -135,8 +144,8 @@
     loads = [
         pltpu.make_async_copy(x_ref, s0.at[:, 2 : 2 + CX, 8 : 8 + CR, :], local_sem.at[0]),
         pltpu.make_async_copy(table_hbm.at[ta], table, local_sem.at[1]),
-        pltpu.make_async_copy(spread_hbm, spread, local_sem.at[2]),
-        pltpu.make_async_copy(phase_hbm, phase_ref, local_sem.at[3]),
+        pltpu.make_async_copy(early_hbm, early, local_sem.at[2]),
+        pltpu.make_async_copy(late_hbm, late, local_sem.at[3]),
         pltpu.make_async_copy(cell_hbm, cell_ref, local_sem.at[4]),
         pltpu.make_async_copy(owner_hbm, owner_ref, local_sem.at[5]),
         pltpu.make_async_copy(diffusivity_hbm, diffusivity, local_sem.at[6]),
@@ -149,18 +158,35 @@
         load.start()
 
     barrier = pltpu.get_barrier_semaphore()
-    for jj in range(N_ROW):
-        for tt in range(2):
-
-            @pl.when(jnp.logical_or(j != jj, ta != tt))
+    sides = (("gx", 0), ("gx", 1), ("row", 0), ("row", 1))
+    for key in sides:
+
+        @pl.when(has[key])
+        def _():
+            pl.semaphore_signal(barrier, 1, device_id=to[key], device_id_type=MESH)
+
+    pl.semaphore_signal(barrier, 1, device_id=(g, j, other), device_id_type=MESH)
+
+    def in_range(distance):
+        return (j - distance >= 0, j - distance), (j + distance < N_ROW, j + distance)
+
+    def announce(distance):
+        for inside, owner in in_range(distance):
+
+            @pl.when(inside)
             def _():
-                pl.semaphore_signal(barrier, 1, device_id=(g, jj, tt), device_id_type=MESH)
-
-    for side in range(2):
-
-        @pl.when(has["gx", side])
-        def _():
-            pl.semaphore_signal(barrier, 1, device_id=to["gx", side], device_id_type=MESH)
+                pl.semaphore_signal(
+                    ready.at[distance // 2], 1, device_id=(g, owner, ta), device_id_type=MESH
+                )
+
+        if distance == 1:
+            pl.semaphore_signal(ready.at[0], 1, device_id=(g, j, other), device_id_type=MESH)
+
+    def heard(distance):
+        count = 1 if distance == 1 else 0
+        for inside, _ in in_range(distance):
+            count = count + jnp.where(inside, 1, 0)
+        pl.semaphore_wait(ready.at[distance // 2], count)
 
     for side in range(2):
 
@@ -239,22 +265,25 @@
             pl.when(has["gx", side])(gx_copy(t, side, c).start)
         ta_copy(t, c).start()
 
-    peers = 2 * N_ROW - 1 + jnp.where(g > 0, 1, 0) + jnp.where(g < n_gx - 1, 1, 0)
+    peers = 1
+    for key in sides:
+        peers = peers + jnp.where(has[key], 1, 0)
     pl.semaphore_wait(barrier, peers)
-
     for c in ORDER:
         send_chunk(0, c)
+    announce(1)
 
     for load in loads[1:]:
         load.wait()
 
     eye = lax.broadcasted_iota(jnp.int32, (STN, STN), 0) == lax.broadcasted_iota(jnp.int32, (STN, STN), 1)
     before = lax.broadcasted_iota(jnp.int32, (STN, STN), 0) < lax.broadcasted_iota(jnp.int32, (STN, STN), 1)
-    owner_across = jnp.broadcast_to(owner_ref[...], (STN, STN)).astype(F32)
+    owners = owner_ref[...]
+    owner_across = jnp.broadcast_to(owners, (STN, STN)).astype(F32)
     owner_down = jnp.sum(jnp.where(eye, owner_across, 0.0), axis=1, keepdims=True)
     same = jnp.logical_and(before, owner_down == owner_across)
     rank = jnp.sum(jnp.where(same, 1.0, 0.0), axis=0, keepdims=True)
-    slot = owner_across[0:1] * float(CAP) + rank
+    slot = ((owners % 2) * HALF + (owners // 2) * CAP).astype(F32) + rank
     slots = lax.broadcasted_iota(jnp.int32, (SLOTS, STN), 0).astype(F32)
     slot_onehot = jnp.where(slots == slot, 1.0, 0.0).astype(BF16)
     station = cell_ref[...]
@@ -321,59 +350,85 @@
         high, low = split(pressure[...])
         both = jnp.dot(place[...], jnp.concatenate([high, low], axis=1), preferred_element_type=F32)
         high, low = split(both[:, :LANES] + both[:, LANES:])
-        z_out[t] = jnp.dot(
-            jnp.concatenate([high, low, high], axis=1), table[...], preferred_element_type=F32
-        ).reshape(N_ROW, CAP, LANES)
+        pieces = jnp.concatenate([high, low, high], axis=1)
+        if t == STEPS - 1:
+            z_late[...] = jnp.dot(pieces, table[t, :, :LANES], preferred_element_type=F32)
+        else:
+            new = jnp.dot(pieces, table[t], preferred_element_type=F32)
+            z_early[...] = new if t == 0 else z_early[...] + new
 
     half = j // (N_ROW // 2)
-    source = (j % (N_ROW // 2)) * 2 + ta
-    groups = ((0, STEPS - 1), (STEPS - 1, 1))
-
-    def z_copy(group, owner):
-        first, count = groups[group]
-        return pltpu.make_async_remote_copy(
-            src_ref=z_out.at[pl.ds(first, count), owner],
-            dst_ref=z_in.at[source, pl.ds(first, count)],
-            send_sem=z_send.at[group, owner],
-            recv_sem=z_recv.at[group, source],
-            device_id=(g, owner, half),
-            device_id_type=MESH,
-        )
-
-    def away(owner):
-        return jnp.logical_or(owner != j, half != ta)
-
-    def z_start(group):
-        for owner in range(N_ROW):
-            pl.when(away(owner))(z_copy(group, owner).start)
-
-        @pl.when(half == ta)
+    source = j % (N_ROW // 2)
+    stages = ((z_early, half_early, sum_early, in_early), (z_late, half_late, sum_late, in_late))
+
+    def half_copy(stage):
+        whole, arrived, _, _ = stages[stage]
+        return pltpu.make_async_remote_copy(
+            src_ref=whole.at[pl.ds(pl.multiple_of(other * HALF, HALF), HALF)],
+            dst_ref=arrived,
+            send_sem=half_send.at[stage],
+            recv_sem=half_recv.at[stage],
+            device_id=(g, j, other),
+            device_id_type=MESH,
+        )
+
+    def z_copy(stage, i):
+        _, _, summed, landing = stages[stage]
+        return pltpu.make_async_remote_copy(
+            src_ref=summed.at[i],
+            dst_ref=landing.at[source],
+            send_sem=z_send.at[stage, i],
+            recv_sem=z_recv.at[stage, source],
+            device_id=(g, 2 * i + ta, half),
+            device_id_type=MESH,
+        )
+
+    def away(i):
+        return jnp.logical_or(2 * i + ta != j, half != ta)
+
+    def z_start(stage):
+        whole, arrived, summed, landing = stages[stage]
+        half_copy(stage).wait_recv()
+        own = whole[pl.ds(pl.multiple_of(ta * HALF, HALF), HALF), :]
+        summed[...] = (own + arrived[...]).reshape(summed.shape)
+        for ahead in range(N_ROW // 2):
+            i = lax.rem(j // 2 + 2 + ahead, N_ROW // 2)
+            pl.when(away(i))(z_copy(stage, i).start)
+
+        @pl.when(jnp.logical_not(away(j // 2)))
         def _():
-            first, count = groups[group]
-            for t in range(first, first + count):
-                z_in[source, t] = z_out[t, j]
-
-    def z_wait(group):
-        first, count = groups[group]
-        for src in range(N_ROW):
+            landing[source] = summed[j // 2]
+
+    def z_wait(stage):
+        _, _, summed, landing = stages[stage]
+        for src in range(N_ROW // 2):
             copy = pltpu.make_async_remote_copy(
-                src_ref=z_out.at[pl.ds(first, count), 0],
-                dst_ref=z_in.at[src, pl.ds(first, count)],
-                send_sem=z_send.at[group, 0],
-                recv_sem=z_recv.at[group, src],
+                src_ref=summed.at[0],
+                dst_ref=landing.at[src],
+                send_sem=z_send.at[stage, 0],
+                recv_sem=z_recv.at[stage, src],
                 device_id=(g, j, other),
                 device_id_type=MESH,
             )
-            mine = jnp.logical_and(half == ta, source == src)
+            mine = jnp.logical_and(
+                jnp.logical_and(half == ta, source == src), j % 2 == ta
+            )
             pl.when(jnp.logical_not(mine))(copy.wait_recv)
 
-    def accumulate(t, start):
-        w = window[t].astype(F32) * 0.125
-        z = jnp.concatenate([z_in[2 * i, t] + z_in[2 * i + 1, t] for i in range(N_ROW // 2)], axis=0)
-        high, low = split(z * w)
-        wide = jnp.dot(jnp.concatenate([high, low], axis=1), spread[...], preferred_element_type=F32)
-        new = phase_ref[t : t + 1, :] * wide[:, :WIDE] + phase_ref[STEPS + t : STEPS + t + 1, :] * wide[:, WIDE:]
-        return new if start is None else start + new
+    w = [window[t].astype(F32) * 0.125 for t in range(STEPS)]
+
+    def accumulate_early():
+        z = in_early[...].reshape(HALF, 2 * LANES)
+        lanes = lax.broadcasted_iota(jnp.int32, (1, 2 * LANES), 1)
+        scale = jnp.where(lanes < 2 * NM, w[0], jnp.where(lanes < 4 * NM, w[1], w[2]))
+        high, low = split(z * scale)
+        pieces = jnp.concatenate([high, low, high], axis=1)
+        return jnp.dot(pieces, early[...], preferred_element_type=F32)
+
+    def accumulate_late():
+        high, low = split(in_late[...].reshape(HALF, LANES) * w[STEPS - 1])
+        pieces = jnp.concatenate([high, low, high], axis=1)
+        return jnp.dot(pieces, late[...], preferred_element_type=F32)
 
     for t in range(STEPS):
         for c in ORDER:
@@ -389,15 +444,19 @@
             step_chunk(t, c)
             if t < STEPS - 1:
                 send_chunk(t + 1, c)
+            elif c == ORDER[1]:
+                z_start(0)
         coefficients(t)
+        if t < STEPS - 1:
+            heard(1 << t)
+        if t < STEPS - 2:
+            announce(2 << t)
         if t == STEPS - 2:
-            z_start(0)
+            half_copy(0).start()
+    half_copy(1).start()
     z_start(1)
     z_wait(0)
-    total = None
-    for t in range(STEPS - 1):
-        total = accumulate(t, total)
-    acc[...] = total
+    acc[...] = accumulate_early()
     for t in range(STEPS):
         for c in range(CHUNKS):
             for side in range(2):
@@ -405,11 +464,12 @@
             ta_copy(t, c).wait_send()
         for side in range(2):
             pl.when(has["row", side])(row_copy(t, side).wait_send)
-    for group in range(2):
-        for owner in range(N_ROW):
-            pl.when(away(owner))(z_copy(group, owner).wait_send)
+    for stage in range(2):
+        half_copy(stage).wait_send()
+        for i in range(N_ROW // 2):
+            pl.when(away(i))(z_copy(stage, i).wait_send)
     z_wait(1)
-    spectra_ref[...] = accumulate(STEPS - 1, acc[...])[:, :COLS]
+    spectra_ref[...] = (acc[...] + accumulate_late())[:, :COLS]
 
 
 def local(n_gx, conserved, diffusivity, axial_speed, coupling, weights, station_cell, owner_row, window):
@@ -435,9 +495,9 @@
             pltpu.VMEM((STEPS, 2, NF, CX, 2, LANES), F32),
             pltpu.VMEM((CX * CR, LANES), F32),
             pltpu.VMEM((SLOTS, CX * CR), BF16),
-            pltpu.VMEM((3 * LANES, LANES), BF16),
-            pltpu.VMEM((2 * LANES, 2 * WIDE), BF16),
-            pltpu.VMEM((2 * STEPS, WIDE), F32),
+            pltpu.VMEM((STEPS, 3 * LANES, 2 * LANES), BF16),
+            pltpu.VMEM((6 * LANES, WIDE), BF16),
+            pltpu.VMEM((3 * LANES, WIDE), BF16),
             pltpu.VMEM((1, STN), jnp.int32),
             pltpu.VMEM((1, STN), jnp.int32),
             pltpu.SMEM((NF,), F32),
@@ -445,9 +505,16 @@
             pltpu.SMEM((NF, NF), F32),
             pltpu.SMEM((NF,), F32),
             pltpu.SMEM((STEPS,), jnp.int32),
-            pltpu.VMEM((STEPS, N_ROW, CAP, LANES), F32),
-            pltpu.VMEM((N_ROW, STEPS, CAP, LANES), F32),
-            pltpu.VMEM((SLOTS // 2, WIDE), F32),
+            pltpu.VMEM((SLOTS, 2 * LANES), F32),
+            pltpu.VMEM((SLOTS, LANES), F32),
+            pltpu.VMEM((HALF, 2 * LANES), F32),
+            pltpu.VMEM((HALF, LANES), F32),
+            pltpu.VMEM((N_ROW // 2, CAP, 2 * LANES), F32),
+            pltpu.VMEM((N_ROW // 2, CAP, LANES), F32),
+            pltpu.VMEM((N_ROW // 2, CAP, 2 * LANES), F32),
+            pltpu.VMEM((N_ROW // 2, CAP, LANES), F32),
+            pltpu.VMEM((HALF, WIDE), F32),
+            pltpu.SemaphoreType.REGULAR((3,)),
             dma((11,)),
             dma((STEPS, 2, CHUNKS)),
             dma((STEPS, 2, CHUNKS)),
@@ -455,8 +522,10 @@
             dma((STEPS, CHUNKS)),
             dma((STEPS, 2)),
             dma((STEPS, 2)),
-            dma((2, N_ROW)),
-            dma((2, N_ROW)),
+            dma((2,)),
+            dma((2,)),
+            dma((2, N_ROW // 2)),
+            dma((2, N_ROW // 2)),
         ],
         compiler_params=pltpu.CompilerParams(
             collective_id=0, has_side_effects=True, vmem_limit_bytes=40 * 1024 * 1024
@@ -474,8 +543,7 @@
                 station_cell.reshape(1, STN),
                 owner_row.reshape(1, STN),
                 jnp.asarray(azimuth_tables()),
-                jnp.asarray(spread_table()),
-                jnp.asarray(phase_rows()),
+                *(jnp.asarray(table) for table in phase_tables()),
             )
         )
     )

time: 48.3 us -> 46.2 us (0.957)
  Pallas kernels: 46 us -> 43.9 us
    pallas_call x1, Pallas kernels: 46 us -> 43.9 us  [local(): pl.pallas_call(functools.partial(kernel, n_gx), out_shape=(jax.ShapeDtype...]
where the time goes in v2:
time: 46.2 us; the launch traced here: 46.1 us
  Pallas kernels  43.9 us (95%)
  local copies, waits for them, and re-layouts  1.55 us (3%)
  between operations  0.64 us (1%)
    pallas_call x1, Pallas kernels, local(): pl.pallas_call(functools.partial(kernel, n_gx), out_shape=(jax.ShapeDtype...  43.9 us
    unnamed x2, local copies, waits for them, and re-layouts  1.55 us

profile of v2, /device:TPU:39, one launch (start us, length us, event | category | flops | bytes accessed | tf_op | source)
XLA Modules:
  0.0 46.1 jit_solution(8216314906857552605)
XLA Ops:
  0.6 43.9 %shard_map.122 = (f32[5,8,32,128]{3,2,1,0:T(8,128)S(1)}, f32[64,1056]{1,0:T(8,128)S(1)}) custom-call(f32[5,8,32,128]{3,2,1,0:T(8,128)} %x_ref.1, f32[5]{0:T(128)} %diffusivity_hbm.1, f32[5]{0:T(128)} %axial_speed_hbm.1, f32[5,5]{1,0:T(8,128)} %coupling_hbm.1, f32[5]{0:T(128)} %weights_hbm.1, s32[4]{0:T(128)} %window_hbm.1, s32[1,32]{1,0:T(1,128)} %bitcast.4, ...), custom_call_target="tpu_custom_call" | custom-call | tf_op jit(solution)/shard_map/pallas_call | solution.py:480
  44.6 0.8 %copy.15 = f32[5,8,32,128]{3,2,1,0:T(8,128)} copy(f32[5,8,32,128]{3,2,1,0:T(8,128)S(1)} %get-tuple-element.8) | data formatting | bytes 1310720
  45.4 0.7 %copy.16 = f32[1,64,1056]{2,1,0:T(8,128)} copy(f32[1,64,1056]{2,1,0:T(8,128)S(1)} %bitcast.3) | data formatting | bytes 540672

commit v3 on v2

--- a/solution.py
+++ b/solution.py
@@ -200,10 +200,6 @@
             for t in range(STEPS):
                 row_in[t, side] = jnp.zeros((NF, CX, 2, LANES), F32)
 
-    loads[0].wait()
-    for f in range(NF):
-        row_out[0, 0, f] = s0[f, 2 : 2 + CX, 8:10, :]
-        row_out[0, 1, f] = s0[f, 2 : 2 + CX, 38:40, :]
 
     def gx_copy(t, side, c):
         rows = pl.ds(8 + 8 * c, 8)
@@ -229,7 +225,7 @@
 
     def row_copy(t, side):
         return pltpu.make_async_remote_copy(
-            src_ref=row_out.at[t, side],
+            src_ref=x_ref.at[:, :, pl.ds((CR - 2) * side, 2), :] if t == 0 else row_out.at[t, side],
             dst_ref=row_in.at[t, 1 - side],
             send_sem=row_send.at[t, side],
             recv_sem=row_recv.at[t, 1 - side],
@@ -259,7 +255,7 @@
 
     def send_chunk(t, c):
         for side, edge in ((0, 0), (1, CHUNKS - 1)):
-            if c == edge:
+            if c == edge and t > 0:
                 pl.when(has["row", side])(row_copy(t, side).start)
         for side in range(2):
             pl.when(has["gx", side])(gx_copy(t, side, c).start)
@@ -269,6 +265,9 @@
     for key in sides:
         peers = peers + jnp.where(has[key], 1, 0)
     pl.semaphore_wait(barrier, peers)
+    for side in range(2):
+        pl.when(has["row", side])(row_copy(0, side).start)
+    loads[0].wait()
     for c in ORDER:
         send_chunk(0, c)
     announce(1)
@@ -470,6 +469,17 @@
             pl.when(away(i))(z_copy(stage, i).wait_send)
     z_wait(1)
     spectra_ref[...] = (acc[...] + accumulate_late())[:, :COLS]
+
+
+def write_out(advanced_ref, spectra_ref, advanced_hbm, spectra_hbm, sem):
+    copies = [
+        pltpu.make_async_copy(advanced_ref, advanced_hbm, sem.at[0]),
+        pltpu.make_async_copy(spectra_ref, spectra_hbm, sem.at[1]),
+    ]
+    for copy in copies:
+        copy.start()
+    for copy in copies:
+        copy.wait()
 
 
 def local(n_gx, conserved, diffusivity, axial_speed, coupling, weights, station_cell, owner_row, window):
@@ -547,6 +557,17 @@
             )
         )
     )
+    advanced, spectra = pl.pallas_call(
+        write_out,
+        out_shape=(
+            jax.ShapeDtypeStruct(advanced.shape, F32),
+            jax.ShapeDtypeStruct(spectra.shape, F32),
+        ),
+        in_specs=[pl.BlockSpec(memory_space=pl.ANY)] * 2,
+        out_specs=(hbm, hbm),
+        compiler_params=pltpu.CompilerParams(vmem_limit_bytes=1024 * 1024),
+        scratch_shapes=[dma((2,))],
+    )(advanced, spectra)
     return advanced, spectra[None]
 
 

time: 46.2 us -> 45.2 us (0.978)
  local copies, waits for them, and re-layouts: 1.55 us -> 0 us
  Pallas kernels: 43.9 us -> 44.4 us
    unnamed x2 -> x0, local copies, waits for them, and re-layouts: 1.55 us -> none
    pallas_call x0 -> x1, Pallas kernels: none -> 0.95 us  [local(): pl.pallas_call(write_out, out_shape=(jax.ShapeDtypeStruct(advanced.shape,...]
where the time goes in v3:
time: 45.2 us; the launch traced here: 45.1 us
  Pallas kernels  44.4 us (98%)
  between operations  0.64 us (1%)
    pallas_call x1, Pallas kernels, local(): pl.pallas_call(functools.partial(kernel, n_gx), out_shape=(jax.ShapeDtype...  43.5 us
    pallas_call x1, Pallas kernels, local(): pl.pallas_call(write_out, out_shape=(jax.ShapeDtypeStruct(advanced.shape,...  0.95 us

profile of v3, /device:TPU:39, one launch (start us, length us, event | category | flops | bytes accessed | tf_op | source)
XLA Modules:
  0.0 45.1 jit_solution(11641752006884961655)
XLA Ops:
  0.6 43.5 %shard_map.122 = (f32[5,8,32,128]{3,2,1,0:T(8,128)S(1)}, f32[64,1056]{1,0:T(8,128)S(1)}) custom-call(f32[5,8,32,128]{3,2,1,0:T(8,128)} %x_ref.1, f32[5]{0:T(128)} %diffusivity_hbm.1, f32[5]{0:T(128)} %axial_speed_hbm.1, f32[5,5]{1,0:T(8,128)} %coupling_hbm.1, f32[5]{0:T(128)} %weights_hbm.1, s32[4]{0:T(128)} %window_hbm.1, s32[1,32]{1,0:T(1,128)} %bitcast.3, ...), custom_call_target="tpu_custom_call" | custom-call | tf_op jit(solution)/shard_map/pallas_call | solution.py:490
  44.1 0.9 %shard_map.123 = (f32[5,8,32,128]{3,2,1,0:T(8,128)}, f32[64,1056]{1,0:T(8,128)}) custom-call(f32[5,8,32,128]{3,2,1,0:T(8,128)S(1)} %get-tuple-element.6.advanced_ref, f32[64,1056]{1,0:T(8,128)S(1)} %get-tuple-element.7.spectra_ref), custom_call_target="tpu_custom_call" | custom-call | tf_op jit(solution)/shard_map/pallas_call | solution.py:560

commit v4 on v3

--- a/solution.py
+++ b/solution.py
@@ -443,8 +443,6 @@
             step_chunk(t, c)
             if t < STEPS - 1:
                 send_chunk(t + 1, c)
-            elif c == ORDER[1]:
-                z_start(0)
         coefficients(t)
         if t < STEPS - 1:
             heard(1 << t)
@@ -452,6 +450,7 @@
             announce(2 << t)
         if t == STEPS - 2:
             half_copy(0).start()
+            z_start(0)
     half_copy(1).start()
     z_start(1)
     z_wait(0)

time: 45.2 us -> 44.7 us (0.989)
  Pallas kernels: 44.4 us -> 43.9 us
    pallas_call x1, Pallas kernels: 43.5 us -> 43 us  [local(): pl.pallas_call(functools.partial(kernel, n_gx), out_shape=(jax.ShapeDtype...]
where the time goes in v4:
time: 44.7 us; the launch traced here: 44.6 us
  Pallas kernels  43.9 us (98%)
  between operations  0.64 us (1%)
    pallas_call x1, Pallas kernels, local(): pl.pallas_call(functools.partial(kernel, n_gx), out_shape=(jax.ShapeDtype...  43 us
    pallas_call x1, Pallas kernels, local(): pl.pallas_call(write_out, out_shape=(jax.ShapeDtypeStruct(advanced.shape,...  0.95 us

profile of v4, /device:TPU:39, one launch (start us, length us, event | category | flops | bytes accessed | tf_op | source)
XLA Modules:
  0.0 44.6 jit_solution(16560574505198202645)
XLA Ops:
  0.6 43.0 %shard_map.122 = (f32[5,8,32,128]{3,2,1,0:T(8,128)S(1)}, f32[64,1056]{1,0:T(8,128)S(1)}) custom-call(f32[5,8,32,128]{3,2,1,0:T(8,128)} %x_ref.1, f32[5]{0:T(128)} %diffusivity_hbm.1, f32[5]{0:T(128)} %axial_speed_hbm.1, f32[5,5]{1,0:T(8,128)} %coupling_hbm.1, f32[5]{0:T(128)} %weights_hbm.1, s32[4]{0:T(128)} %window_hbm.1, s32[1,32]{1,0:T(1,128)} %bitcast.3, ...), custom_call_target="tpu_custom_call" | custom-call | tf_op jit(solution)/shard_map/pallas_call | solution.py:489
  43.6 0.9 %shard_map.123 = (f32[5,8,32,128]{3,2,1,0:T(8,128)}, f32[64,1056]{1,0:T(8,128)}) custom-call(f32[5,8,32,128]{3,2,1,0:T(8,128)S(1)} %get-tuple-element.6.advanced_ref, f32[64,1056]{1,0:T(8,128)S(1)} %get-tuple-element.7.spectra_ref), custom_call_target="tpu_custom_call" | custom-call | tf_op jit(solution)/shard_map/pallas_call | solution.py:559
